TPU v7x, 32 devices: a whole 2x2x4 slice. The times are simulated.
32 devices in a mesh: grp: 4 (over y, x), aux: 8 (over z, core).
Axes of the slice: x: 2, y: 2, z: 4, core: 2. Of those that a mesh axis runs over, the one named last changes fastest.
Arguments:
- integrals: bfloat16 [2048, 32, 512], P('aux', 'grp'), may hold values from -0.75 to 0.75
- metric: bfloat16 [2048, 2048], replicated, may hold values from -0.125 to 0.125
- occupied_energy: float32 [32], replicated, may hold values from -2 to -0.5
- virtual_energy: float32 [512], replicated, may hold values from 0.2 to 3
- plan: int32 [4, 8], replicated, may hold values from 0 to 3
Outputs:
- density: bfloat16 [2048, 32, 512], P('aux', 'grp')
All inputs are finite; a program needn't handle non-finite values.
Results may differ from a plain program's by a relative error of at most 0.0053.
Values may be sent and summed in bfloat16 or wider, within the bound.
A program may use at most 128 MiB of HBM per device.

v0:
```python
import jax
import jax.numpy as jnp
from jax import lax
from jax.sharding import PartitionSpec as P


def pair_term(own_block, partner, own_energy, partner_energy, virtual_energy):
    coulomb = jnp.einsum("qia,qjb->ijab", own_block, partner, preferred_element_type=jnp.float32)
    denominator = (
        own_energy[:, None, None, None]
        + partner_energy[None, :, None, None]
        - virtual_energy[None, None, :, None]
        - virtual_energy[None, None, None, :]
    )
    amplitude = ((2.0 * coulomb - jnp.swapaxes(coulomb, 2, 3)) / denominator).astype(jnp.bfloat16)
    return jnp.einsum("ijab,qjb->qia", amplitude, partner, preferred_element_type=jnp.float32)


def body(integrals, metric, occupied_energy, virtual_energy, plan):
    shards = lax.axis_size("aux")
    per_device = integrals.shape[1] // shards
    aux_rows = metric.shape[0]
    aux_place = lax.axis_index("aux")
    block_index = lax.axis_index("grp") * shards + aux_place
    received = lax.all_to_all(integrals, "aux", split_axis=1, concat_axis=0, tiled=True)
    flattened = received.reshape(aux_rows, per_device * received.shape[2])
    own_block = jnp.dot(metric, flattened, preferred_element_type=jnp.float32)
    own_block = own_block.astype(jnp.bfloat16).reshape(received.shape)
    own_energy = lax.dynamic_slice_in_dim(occupied_energy, block_index * per_device, per_device)
    density_sum = jnp.zeros(own_block.shape, jnp.float32)
    gathered_all = lax.all_gather(own_block, "grp", axis=1, tiled=True)
    for step_index in range(plan.shape[0]):
        owner_group = lax.dynamic_index_in_dim(plan[step_index], aux_place, 0, keepdims=False)
        partner = lax.dynamic_slice_in_dim(gathered_all, owner_group * per_device, per_device, 1)
        first_index = (owner_group * shards + aux_place) * per_device
        partner_energy = lax.dynamic_slice_in_dim(occupied_energy, first_index, per_device)
        density_sum = density_sum + pair_term(
            own_block, partner, own_energy, partner_energy, virtual_energy
        )
    density = density_sum.astype(jnp.bfloat16)
    return lax.all_to_all(density, "aux", split_axis=0, concat_axis=1, tiled=True)


def solution(mesh):
    in_specs = (P("aux", "grp", None), P(), P(), P(), P())
    out_specs = P("aux", "grp", None)
    return jax.shard_map(body, mesh=mesh, in_specs=in_specs, out_specs=out_specs, check_vma=False)
```

profile of v0, /device:TPU:0, one launch (start us, length us, event | category | flops | bytes accessed | tf_op | source)
XLA Modules:
  0.0 309.3 jit_solution(2599807200731962696)
XLA Ops:
  6.5 2.4 copy.41
  9.0 55.3 %all_to_all.33 = bf16[256,8,512]{2,0,1:T(8,128)(2,1)S(1)} all-to-all(bf16[256,8,512]{2,0,1:T(8,128)(2,1)S(1)} %copy.41), channel_id=1, replica_groups=mesh['grp'=4,'aux'=8] {'aux'}, dimensions={1} | all-to-all | bytes 4194304 | tf_op jit(solution)/shard_map/all_to_all | solution.py:25
  64.3 5.7 %convolution_convert_fusion = bf16[2048,512]{1,0:T(8,128)(2,1)} fusion(bf16[2048,2048]{1,0:T(8,128)(2,1)S(1)} %copy-done.16, bf16[2048,512]{1,0:T(8,128)(2,1)S(1)} %bitcast.123), kind=kOutput, calls=%fused_computation.1 | convolution fusion | flops 4296015872 | bytes 12582912 | tf_op jit(solution)/shard_map/dot_general | solution.py:27
  87.1 69.4 %all-gather.3.cloned.1.call-done = bf16[2048,2048]{1,0:T(8,128)(2,1)} async-done(((bf16[2048,512]{1,0:T(8,128)(2,1)}), bf16[2048,2048]{1,0:T(8,128)(2,1)}) %all-gather.3.cloned.1.call-update) | async-done | bytes 8388624 | tf_op jit(solution)/shard_map/all_gather | solution.py:31
  156.5 14.6 %reshape.285 = bf16[2048,4,512]{2,1,0:T(4,128)(2,1)} reshape(bf16[2048,2048]{1,0:T(8,128)(2,1)} %all-gather.3.cloned.1.call-done) | data formatting | bytes 16777216 | tf_op jit(solution)/shard_map/all_gather | solution.py:31
  171.1 27.4 %constant_dynamic-slice_fusion = (bf16[2048,1,512]{2,1,0:T(2,128)(2,1)}, bf16[2048,1,512]{2,1,0:T(2,128)(2,1)}, bf16[2048,1,512]{2,1,0:T(2,128)(2,1)S(1)}, bf16[2048,1,512]{2,1,0:T(2,128)(2,1)}) fusion(bf16[2048,4,512]{2,1,0:T(4,128)(2,1)} %reshape.285, s32[]{:T(128)S(6)} %select_n.42, s32[]{:T(128)S(6)} %select_n.40, s32[]{:T(128)S(6)} %select_n.38, ...), kind=kLoop, calls=%fused_computation.36 | loop fusion | bytes 16777232 | tf_op jit(solution)/shard_map/dynamic_slice | solution.py:34
  198.5 2.0 copy-done.4
  201.7 1.3 copy.46
  203.1 3.5 %fusion.10 = f32[512,512]{1,0:T(8,128)S(1)} fusion(bf16[2048,512]{1,0:T(8,128)(2,1)S(1)} %copy-done, bf16[2048,1,512]{2,1,0:T(2,128)(2,1)} %get-tuple-element.8), kind=kOutput, calls=%fused_computation.20 | convolution fusion | flops 1073741824 | bytes 5242880 | tf_op jit(solution)/shard_map/qia,qjb->ijab/dot_general | solution.py:8
  206.6 1.3 copy.43
  207.9 3.5 %fusion.14 = f32[512,512]{1,0:T(8,128)S(1)} fusion(bf16[2048,512]{1,0:T(8,128)(2,1)S(1)} %copy-done, bf16[2048,1,512]{2,1,0:T(2,128)(2,1)} %get-tuple-element.6), kind=kOutput, calls=%fused_computation.24 | convolution fusion | flops 1073741824 | bytes 5242880 | tf_op jit(solution)/shard_map/qia,qjb->ijab/dot_general | solution.py:8
  211.4 1.3 copy.49
  212.7 3.5 %fusion.15 = f32[512,512]{1,0:T(8,128)S(1)} fusion(bf16[2048,512]{1,0:T(8,128)(2,1)S(1)} %copy-done, bf16[2048,1,512]{2,1,0:T(2,128)(2,1)} %get-tuple-element.5), kind=kOutput, calls=%fused_computation.25 | convolution fusion | flops 1073741824 | bytes 5242880 | tf_op jit(solution)/shard_map/qia,qjb->ijab/dot_general | solution.py:8
  216.2 1.4 copy.52
  217.5 4.4 %fusion.11 = f32[2048,512]{1,0:T(8,128)S(1)} fusion(bf16[2048,1,512]{2,1,0:T(2,128)(2,1)} %copy-done.4, f32[512,512]{1,0:T(8,128)} %copy-done.10, f32[512,512]{0,1:T(8,128)} %copy.46, f32[512]{0:T(512)S(1)} %copy-done.14, f32[512]{0:T(512)S(1)} %get-tuple-element.10), kind=kOutput, calls=%fused_computation.21 | convolution fusion | flops 1075052544 | bytes 8392704 | tf_op jit(solution)/shard_map/ijab,qjb->qia/dot_general | solution.py:16
  222.2 1.5 fusion.9
  225.0 1.5 fusion.13
  227.5 1.8 fusion
  229.8 3.1 %reduce = bf16[2048,512]{1,0:T(8,128)(2,1)} reduce(bf16[2048,1,512]{2,0,1:T(8,128)(2,1)S(1)} %fusion, bf16[]{:T(256)} %broadcast.215), dimensions={1}, to_apply=%copy.53.reduce_sub_computation | reduce | bytes 4194306 | tf_op jit(solution)/shard_map/convert_element_type | solution.py:40
  232.9 6.3 %reshape.286 = bf16[8,2,65536]{2,1,0:T(2,128)(2,1)} reshape(bf16[2048,512]{1,0:T(8,128)(2,1)} %reduce) | data formatting | bytes 4194304
  239.2 53.7 %all_to_all.34 = bf16[8,2,65536]{2,1,0:T(2,128)(2,1)S(1)} all-to-all(bf16[8,2,65536]{2,1,0:T(2,128)(2,1)} %reshape.286), channel_id=1, replica_groups=mesh['grp'=4,'aux'=8] {'aux'}, dimensions={0} | all-to-all | bytes 4194304 | tf_op jit(solution)/shard_map/all_to_all | solution.py:41
  292.9 4.3 %reshape.287 = bf16[2048,1,512]{2,1,0:T(2,128)(2,1)} reshape(bf16[8,2,65536]{2,1,0:T(2,128)(2,1)S(1)} %all_to_all.34) | data formatting | bytes 4194304
  297.2 2.8 copy.55
  300.0 2.5 copy.54
  (42 shorter events, 6.4 us)
Async XLA Ops:
  6.5 150.0 %all-gather.3.cloned.1.call-start = ((), (), s32[]{:S(2)}) async-start(), calls=%async_computation.2 | async-start | bytes 10485760 | tf_op jit(solution)/shard_map/all_gather | solution.py:31
  6.5 57.7 %copy-start.16 = (bf16[2048,2048]{1,0:T(8,128)(2,1)S(1)}, bf16[2048,2048]{1,0:T(8,128)(2,1)}, u32[]{:S(2)}) copy-start(bf16[2048,2048]{1,0:T(8,128)(2,1)} %param.6) | copy-start | bytes 25165828
  64.3 5.7 %copy-start.15 = (s32[4,8]{1,0:T(4,128)S(1)}, s32[4,8]{1,0:T(4,128)}, u32[]{:S(2)}) copy-start(s32[4,8]{1,0:T(4,128)} %param.9) | copy-start | bytes 388
  64.3 14.6 %copy-start.13 = (f32[32]{0:T(128)S(1)}, f32[32]{0:T(128)}, u32[]{:S(2)}) copy-start(f32[32]{0:T(128)} %param.7) | copy-start | bytes 388
  64.3 22.8 %copy-start.14 = (f32[512]{0:T(512)S(1)}, f32[512]{0:T(512)}, u32[]{:S(2)}) copy-start(f32[512]{0:T(512)} %param.8) | copy-start | bytes 6148
  171.1 29.4 %copy-start = (bf16[2048,512]{1,0:T(8,128)(2,1)S(1)}, bf16[2048,512]{1,0:T(8,128)(2,1)}, u32[]{:S(2)}) copy-start(bf16[2048,512]{1,0:T(8,128)(2,1)} %convolution_convert_fusion) | copy-start | bytes 6291460
  198.5 2.0 copy-start.4
  201.7 1.3 copy-start.10
  206.5 1.3 copy-start.8
  211.3 1.3 copy-start.6
  217.5 4.4 %copy-start.3 = (bf16[2048,1,512]{2,1,0:T(2,128)(2,1)S(1)}, bf16[2048,1,512]{2,1,0:T(2,128)(2,1)}, u32[]{:S(2)}) copy-start(bf16[2048,1,512]{2,1,0:T(2,128)(2,1)} %get-tuple-element.8) | copy-start | bytes 6291460
  217.5 4.4 %copy-start.9 = (f32[512,512]{1,0:T(8,128)S(1)}, f32[512,512]{1,0:T(8,128)}, u32[]{:S(2)}) copy-start(f32[512,512]{1,0:T(8,128)} %copy-done.8) | copy-start | bytes 3145732
  217.5 4.7 %copy-start.12 = (f32[512,512]{0,1:T(8,128)S(1)}, f32[512,512]{0,1:T(8,128)}, u32[]{:S(2)}) copy-start(f32[512,512]{0,1:T(8,128)} %copy.43) | copy-start | bytes 3145732
  222.2 2.2 copy-start.2
  222.2 2.5 copy-start.7
  222.2 2.8 copy-start.11
  225.0 2.2 copy-start.1
  225.0 2.5 copy-start.5
Sparse Core Ops, SparseCore 0:
  70.1 86.3 all-gather.2
where the time goes:
time: 310 us; the launch traced here: 309 us
  blocking collectives  109 us (35%)
  local copies, waits for them, and re-layouts  72.6 us (23%)
  waiting for transfers between devices  69.4 us (22%)
  between operations  28.6 us (9%)
  matrix products  26.5 us (9%)
  other arithmetic  3.11 us (1%)
    all_gather x1, waiting for transfers between devices, body(): gathered_all = lax.all_gather(own_block, 'grp', axis=1, tiled=True)  69.4 us
    all_to_all x1, blocking collectives, body(): lax.all_to_all(integrals, 'aux', split_axis=1, concat_axis=0, tiled=True)  55.3 us
    all_to_all x1, blocking collectives, body(): lax.all_to_all(density, 'aux', split_axis=0, concat_axis=1, tiled=True)  53.7 us
    dynamic_slice x1, local copies, waits for them, and re-layouts, body(): lax.dynamic_slice_in_dim(gathered_all, owner_group * per_device, per_devi...  27.4 us
    unnamed x38, local copies, waits for them, and re-layouts  20.3 us
    all_gather x1, local copies, waits for them, and re-layouts, body(): gathered_all = lax.all_gather(own_block, 'grp', axis=1, tiled=True)  14.6 us
    dot_general x4, matrix products, pair_term(): jnp.einsum('qia,qjb->ijab', own_block, partner, preferred_element_type=jn...  11.7 us
    dot_general x4, matrix products, pair_term(): jnp.einsum('ijab,qjb->qia', amplitude, partner, preferred_element_type=jn...  9.21 us
  transfers between devices with their start and end apart: 1, of which 1 were waited for; matrix products, arithmetic and copies ran while one was open for 1% of the time, Pallas kernels for 0%

commit v1 on v0

v1 whole, which is shorter than its diff:
```python
import functools

import jax
import jax.numpy as jnp
from jax import lax
from jax.experimental import pallas as pl
from jax.experimental.pallas import tpu as pltpu
from jax.sharding import PartitionSpec as P

MESH = pl.DeviceIdType.MESH
CHUNK = 128


def dot(left, right):
    return lax.dot_general(left, right, (((1,), (0,)), ((), ())), preferred_element_type=jnp.float32)


def kernel(n, shards, x, metric, vrow, vcol, occ, plan, y, mvm, recv, blocks, own_t, exch, amp, dens,
           msem, in_send, in_recv, in_local, g_send, g_recv, f_send, f_recv, out_send, out_recv, out_local):
    grp = lax.axis_index("grp")
    me = lax.axis_index("aux")
    chunks, rows, width = x.shape[1], x.shape[2], x.shape[3]
    aux_rows = metric.shape[0]
    nvirt = vrow.shape[1]
    relay = n == 4
    steps = plan.shape[0]

    def aux_at(d):
        return lax.rem(me + d, shards)

    if relay:
        one = grp + 1 - 2 * lax.rem(grp, 2)
        two = lax.rem(grp + 2, 4)
        target = [grp, one, two, lax.rem(one + 2, 4)]
        source = target
    else:
        target = [lax.rem(grp + d, n) for d in range(n)]
        source = [lax.rem(grp + n - d, n) for d in range(n)]

    load = pltpu.make_async_copy(metric, mvm, msem)
    load.start()

    barrier = pltpu.get_barrier_semaphore()

    @pl.loop(1, shards)
    def _(d):
        pl.semaphore_signal(barrier, inc=1, device_id=(grp, aux_at(d)), device_id_type=MESH)

    for d in range(1, n):
        pl.semaphore_signal(barrier, inc=1, device_id=(target[d], me), device_id_type=MESH)
    pl.semaphore_wait(barrier, shards - 1 + n - 1)

    def in_copy(k, d):
        return pltpu.make_async_remote_copy(
            src_ref=x.at[aux_at(d), k], dst_ref=recv.at[k, me], send_sem=in_send.at[k, d],
            recv_sem=in_recv.at[k, d], device_id=(grp, aux_at(d)), device_id_type=MESH)

    def in_own(k):
        return pltpu.make_async_copy(x.at[me, k], recv.at[k, me], in_local.at[k])

    def send_in(k):
        in_own(k).start()

        @pl.loop(1, shards)
        def _(d):
            in_copy(k, d).start()

    def wait_in(k):
        in_own(k).wait()

        @pl.loop(1, shards)
        def _(d):
            place = lax.rem(me + shards - d, shards)
            pltpu.make_async_remote_copy(
                src_ref=x.at[place, k], dst_ref=recv.at[k, place], send_sem=in_send.at[k, d],
                recv_sem=in_recv.at[k, d], device_id=(grp, aux_at(d)), device_id_type=MESH).wait_recv()

    def g_copy(k, d):
        return pltpu.make_async_remote_copy(
            src_ref=blocks.at[0, k], dst_ref=blocks.at[d, k], send_sem=g_send.at[d, k],
            recv_sem=g_recv.at[d, k], device_id=(target[d], me), device_id_type=MESH)

    half = aux_rows // 2

    def f_copy(k, way):
        part = pl.ds(way * half, half)
        return pltpu.make_async_remote_copy(
            src_ref=blocks.at[1 + way, k, part], dst_ref=blocks.at[3, k, part], send_sem=f_send.at[way, k],
            recv_sem=f_recv.at[way, k], device_id=(target[2 - way], me), device_id_type=MESH)

    direct = (1, 2) if relay else tuple(range(1, n))

    def forward(k):
        for d in (1, 2):
            g_copy(k, d).wait_recv()
            f_copy(k, d - 1).start()

    tile = min(512, aux_rows)
    send_in(0)
    if chunks > 1:
        send_in(1)
    for k in range(chunks):
        wait_in(k)
        if k + 2 < chunks:
            send_in(k + 2)
        if k == 0:
            load.wait()

        @pl.loop(0, aux_rows // tile)
        def _(t):
            at = pl.ds(pl.multiple_of(t * tile, tile), tile)
            part = dot(mvm[at, :], recv[k].reshape(aux_rows, width))
            blocks[0, k, at, :] = part.astype(jnp.bfloat16)

        for d in direct:
            g_copy(k, d).start()
        if relay and k >= 1:
            forward(k - 1)
        own_t[k * width:(k + 1) * width, :] = blocks[0, k].T

    def pair(d):
        per = max(1, min(256 // width, chunks))
        for k in range(0, chunks, per):
            right = jnp.concatenate([blocks[d, k + m] for m in range(per)], axis=1)
            exch[:, k * width:(k + per) * width] = dot(own_t[...], right)
        weight = jnp.float32(0.0)
        for s in range(steps):
            weight = weight + jnp.where(plan[s, me] == source[d], jnp.float32(1.0), jnp.float32(0.0))
        shift = occ[grp * shards + me] + occ[source[d] * shards + me]
        value = exch[...]
        below = shift - vcol[...] - vrow[...]
        value = weight * ((2.0 * value.T - value) / below)
        amp[d * nvirt:(d + 1) * nvirt, :] = value.astype(jnp.bfloat16)

    pair(0)
    if relay:
        forward(chunks - 1)
        pair(1)
        pair(2)
        for k in range(chunks):
            for way in (0, 1):
                f_copy(k, way).wait_recv()
        pair(3)
    else:
        for d in direct:
            for k in range(chunks):
                g_copy(k, d).wait_recv()
            pair(d)

    def density(d):
        at = pl.ds(pl.multiple_of(aux_at(d) * rows, rows), rows)
        left = jnp.concatenate([blocks[s, k, at, :] for s in range(n) for k in range(chunks)], axis=1)
        dens[d] = dot(left, amp[...]).astype(jnp.bfloat16)

    def out_copy(d):
        return pltpu.make_async_remote_copy(
            src_ref=dens.at[d], dst_ref=y.at[me], send_sem=out_send.at[d], recv_sem=out_recv.at[d],
            device_id=(grp, aux_at(d)), device_id_type=MESH)

    @pl.loop(1, shards)
    def _(d):
        density(d)
        out_copy(d).start()

    density(0)
    own_out = pltpu.make_async_copy(dens.at[0], y.at[me], out_local)
    own_out.start()
    own_out.wait()

    for k in range(chunks):
        @pl.loop(1, shards)
        def _(d):
            in_copy(k, d).wait_send()

        for d in direct:
            g_copy(k, d).wait_send()
        if relay:
            for way in (0, 1):
                f_copy(k, way).wait_send()

    @pl.loop(1, shards)
    def _(d):
        place = lax.rem(me + shards - d, shards)
        out_copy(d).wait_send()
        pltpu.make_async_remote_copy(
            src_ref=dens.at[d], dst_ref=y.at[place], send_sem=out_send.at[d], recv_sem=out_recv.at[d],
            device_id=(grp, aux_at(d)), device_id_type=MESH).wait_recv()


def body(integrals, metric, occupied_energy, virtual_energy, plan):
    n, shards = lax.axis_size("grp"), lax.axis_size("aux")
    rows, places, nvirt = integrals.shape
    aux_rows = metric.shape[0]
    width = CHUNK if nvirt % CHUNK == 0 else nvirt
    chunks = nvirt // width
    x = integrals.reshape(rows, shards, chunks, width).transpose(1, 2, 0, 3)
    any_space = pl.BlockSpec(memory_space=pl.ANY)
    vmem = pl.BlockSpec(memory_space=pltpu.VMEM)
    smem = pl.BlockSpec(memory_space=pltpu.SMEM)
    dma = pltpu.SemaphoreType.DMA
    flops = 2 * aux_rows * nvirt * (aux_rows + 2 * n * nvirt)
    y = pl.pallas_call(
        functools.partial(kernel, n, shards),
        out_shape=jax.ShapeDtypeStruct((shards, rows, nvirt), jnp.bfloat16),
        in_specs=[any_space, any_space, vmem, vmem, smem, smem],
        out_specs=any_space,
        scratch_shapes=[
            pltpu.VMEM((aux_rows, aux_rows), jnp.bfloat16),
            pltpu.VMEM((chunks, shards, rows, width), jnp.bfloat16),
            pltpu.VMEM((n, chunks, aux_rows, width), jnp.bfloat16),
            pltpu.VMEM((nvirt, aux_rows), jnp.bfloat16),
            pltpu.VMEM((nvirt, nvirt), jnp.float32),
            pltpu.VMEM((n * nvirt, nvirt), jnp.bfloat16),
            pltpu.VMEM((shards, rows, nvirt), jnp.bfloat16),
            dma, dma((chunks, shards)), dma((chunks, shards)), dma((chunks,)),
            dma((n, chunks)), dma((n, chunks)), dma((2, chunks)), dma((2, chunks)),
            dma((shards,)), dma((shards,)), dma,
        ],
        compiler_params=pltpu.CompilerParams(
            collective_id=0, has_side_effects=True, vmem_limit_bytes=56 * 1024 * 1024),
        cost_estimate=pl.CostEstimate(
            flops=flops, bytes_accessed=2 * aux_rows * aux_rows, transcendentals=0),
    )(x, metric, virtual_energy.reshape(1, nvirt), virtual_energy.reshape(nvirt, 1), occupied_energy, plan)
    return y.transpose(1, 0, 2)


def solution(mesh):
    in_specs = (P("aux", "grp", None), P(), P(), P(), P())
    out_specs = P("aux", "grp", None)
    return jax.shard_map(body, mesh=mesh, in_specs=in_specs, out_specs=out_specs, check_vma=False)
```

time: 310 us -> 154 us (0.50)
  the two profiles are of different devices: /device:TPU:0 before, /device:TPU:25 now
where the time goes in v1:
time: 154 us; the launch traced here: 153 us
  Pallas kernels  144 us (94%)
  local copies, waits for them, and re-layouts  9.35 us (6%)
    pallas_call x1, Pallas kernels, body(): pl.pallas_call(functools.partial(kernel, n, shards), out_shape=jax.ShapeD...  144 us
    transpose x1, local copies, waits for them, and re-layouts, body(): return y.transpose(1, 0, 2)  4.07 us
    reshape x1, local copies, waits for them, and re-layouts, body(): x = integrals.reshape(rows, shards, chunks, width).transpose(1, 2, 0, 3)  3.72 us

profile of v1, /device:TPU:25, one launch (start us, length us, event | category | flops | bytes accessed | tf_op | source)
XLA Modules:
  0.0 153.5 jit_solution(14193159289946660172)
XLA Ops:
  0.0 1.6 %copy.8.vcol = f32[512,1]{1,0:T(8,128)} copy(f32[512,1]{0,1:T(1,128)} %bitcast.10) | data formatting | bytes 4096 | tf_op jit(solution)/shard_map/reshape | solution.py:223
  1.6 3.7 %copy.11 = bf16[256,8,4,128]{3,0,2,1:T(8,128)(2,1)} copy(bf16[256,8,4,128]{3,1,2,0:T(8,128)(2,1)} %bitcast.7) | data formatting | bytes 4194304 | tf_op jit(solution)/shard_map/reshape | solution.py:196
  5.3 144.1 %shard_map.55 = bf16[8,256,512]{2,1,0:T(8,128)(2,1)} custom-call(bf16[8,4,256,128]{3,2,1,0:T(8,128)(2,1)} %bitcast.9, bf16[2048,2048]{1,0:T(8,128)(2,1)} %metric.1, f32[1,512]{1,0:T(1,128)} %bitcast.11, f32[512,1]{1,0:T(8,128)} %copy.8.vcol, f32[32]{0:T(128)} %occ.1, s32[4,8]{1,0:T(4,128)} %plan.1), custom_call_target="tpu_custom_call" | custom-call | flops 12884901888 | bytes 8388608 | tf_op jit(solution)/shard_map/pallas_call | solution.py:202
  149.4 4.1 %copy.9 = bf16[256,8,512]{2,1,0:T(8,128)(2,1)} copy(bf16[256,8,512]{2,0,1:T(8,128)(2,1)} %bitcast.8) | data formatting | bytes 4194304 | tf_op jit(solution)/shard_map/transpose | solution.py:224

commit v2 on v1

--- a/solution.py
+++ b/solution.py
@@ -9,13 +9,14 @@
 
 MESH = pl.DeviceIdType.MESH
 CHUNK = 128
+WINDOW = 3
 
 
 def dot(left, right):
     return lax.dot_general(left, right, (((1,), (0,)), ((), ())), preferred_element_type=jnp.float32)
 
 
-def kernel(n, shards, x, metric, vrow, vcol, occ, plan, y, mvm, recv, blocks, own_t, exch, amp, dens,
+def kernel(n, shards, x, metric, vrow, occ, plan, y, mvm, recv, blocks, own_t, exch, vsum, amp, dens,
            msem, in_send, in_recv, in_local, g_send, g_recv, f_send, f_recv, out_send, out_recv, out_local):
     grp = lax.axis_index("grp")
     me = lax.axis_index("aux")
@@ -58,12 +59,25 @@
     def in_own(k):
         return pltpu.make_async_copy(x.at[me, k], recv.at[k, me], in_local.at[k])
 
-    def send_in(k):
-        in_own(k).start()
-
-        @pl.loop(1, shards)
-        def _(d):
-            in_copy(k, d).start()
+    parity = lax.rem(me, 2)
+    per_class = shards // 2
+
+    def class_loop(odd, act):
+        @pl.loop(0, per_class)
+        def _(e):
+            d = 2 * lax.rem(e + per_class // 2, per_class) + (1 - parity if odd else parity)
+
+            @pl.when(d != 0)
+            def _():
+                act(d)
+
+    def send_step(i):
+        class_loop(i // chunks, lambda d: in_copy(i % chunks, d).start())
+
+    def send_after(k):
+        class_loop(0, lambda d: in_copy(k, d).wait_send())
+        for i in range(k + WINDOW, 2 * chunks if k == chunks - 1 else k + WINDOW + 1):
+            send_step(i)
 
     def wait_in(k):
         in_own(k).wait()
@@ -96,13 +110,24 @@
             f_copy(k, d - 1).start()
 
     tile = min(512, aux_rows)
-    send_in(0)
-    if chunks > 1:
-        send_in(1)
+    for k in range(chunks):
+        in_own(k).start()
+    for i in range(WINDOW):
+        send_step(i)
+    vsum[...] = vrow[...] + jnp.broadcast_to(vrow[...], (nvirt, nvirt)).T
+
+    @pl.when(parity == 1)
+    def _():
+        for k in range(chunks):
+            send_after(k)
+
     for k in range(chunks):
         wait_in(k)
-        if k + 2 < chunks:
-            send_in(k + 2)
+
+        @pl.when(parity == 0)
+        def _():
+            send_after(k)
+
         if k == 0:
             load.wait()
 
@@ -128,7 +153,7 @@
             weight = weight + jnp.where(plan[s, me] == source[d], jnp.float32(1.0), jnp.float32(0.0))
         shift = occ[grp * shards + me] + occ[source[d] * shards + me]
         value = exch[...]
-        below = shift - vcol[...] - vrow[...]
+        below = shift - vsum[...]
         value = weight * ((2.0 * value.T - value) / below)
         amp[d * nvirt:(d + 1) * nvirt, :] = value.astype(jnp.bfloat16)
 
@@ -157,8 +182,9 @@
             src_ref=dens.at[d], dst_ref=y.at[me], send_sem=out_send.at[d], recv_sem=out_recv.at[d],
             device_id=(grp, aux_at(d)), device_id_type=MESH)
 
-    @pl.loop(1, shards)
-    def _(d):
+    @pl.loop(0, shards - 1)
+    def _(t):
+        d = 1 + lax.rem(t + shards // 2 - 1, shards - 1)
         density(d)
         out_copy(d).start()
 
@@ -168,10 +194,7 @@
     own_out.wait()
 
     for k in range(chunks):
-        @pl.loop(1, shards)
-        def _(d):
-            in_copy(k, d).wait_send()
-
+        class_loop(1, lambda d: in_copy(k, d).wait_send())
         for d in direct:
             g_copy(k, d).wait_send()
         if relay:
@@ -202,13 +225,14 @@
     y = pl.pallas_call(
         functools.partial(kernel, n, shards),
         out_shape=jax.ShapeDtypeStruct((shards, rows, nvirt), jnp.bfloat16),
-        in_specs=[any_space, any_space, vmem, vmem, smem, smem],
+        in_specs=[any_space, any_space, vmem, smem, smem],
         out_specs=any_space,
         scratch_shapes=[
             pltpu.VMEM((aux_rows, aux_rows), jnp.bfloat16),
             pltpu.VMEM((chunks, shards, rows, width), jnp.bfloat16),
             pltpu.VMEM((n, chunks, aux_rows, width), jnp.bfloat16),
             pltpu.VMEM((nvirt, aux_rows), jnp.bfloat16),
+            pltpu.VMEM((nvirt, nvirt), jnp.float32),
             pltpu.VMEM((nvirt, nvirt), jnp.float32),
             pltpu.VMEM((n * nvirt, nvirt), jnp.bfloat16),
             pltpu.VMEM((shards, rows, nvirt), jnp.bfloat16),
@@ -220,7 +244,7 @@
             collective_id=0, has_side_effects=True, vmem_limit_bytes=56 * 1024 * 1024),
         cost_estimate=pl.CostEstimate(
             flops=flops, bytes_accessed=2 * aux_rows * aux_rows, transcendentals=0),
-    )(x, metric, virtual_energy.reshape(1, nvirt), virtual_energy.reshape(nvirt, 1), occupied_energy, plan)
+    )(x, metric, virtual_energy.reshape(1, nvirt), occupied_energy, plan)
     return y.transpose(1, 0, 2)
 
 

time: 154 us -> 128 us (0.83)
  the two profiles are of different devices: /device:TPU:25 before, /device:TPU:0 now
where the time goes in v2:
time: 128 us; the launch traced here: 127 us
  Pallas kernels  120 us (94%)
  local copies, waits for them, and re-layouts  7.79 us (6%)
    pallas_call x1, Pallas kernels, body(): pl.pallas_call(functools.partial(kernel, n, shards), out_shape=jax.ShapeD...  120 us
    transpose x1, local copies, waits for them, and re-layouts, body(): return y.transpose(1, 0, 2)  4.07 us
    reshape x1, local copies, waits for them, and re-layouts, body(): x = integrals.reshape(rows, shards, chunks, width).transpose(1, 2, 0, 3)  3.72 us

profile of v2, /device:TPU:0, one launch (start us, length us, event | category | flops | bytes accessed | tf_op | source)
XLA Modules:
  0.0 127.5 jit_solution(2713365175521145999)
XLA Ops:
  0.0 3.7 %copy.10 = bf16[256,8,4,128]{3,0,2,1:T(8,128)(2,1)} copy(bf16[256,8,4,128]{3,1,2,0:T(8,128)(2,1)} %bitcast.6) | data formatting | bytes 4194304 | tf_op jit(solution)/shard_map/reshape | solution.py:219
  3.7 119.7 %shard_map.55 = bf16[8,256,512]{2,1,0:T(8,128)(2,1)} custom-call(bf16[8,4,256,128]{3,2,1,0:T(8,128)(2,1)} %bitcast.8, bf16[2048,2048]{1,0:T(8,128)(2,1)} %metric.1, f32[1,512]{1,0:T(1,128)} %bitcast.9, f32[32]{0:T(128)} %occ.1, s32[4,8]{1,0:T(4,128)} %plan.1), custom_call_target="tpu_custom_call" | custom-call | flops 12884901888 | bytes 8388608 | tf_op jit(solution)/shard_map/pallas_call | solution.py:225
  123.4 4.1 %copy.8 = bf16[256,8,512]{2,1,0:T(8,128)(2,1)} copy(bf16[256,8,512]{2,0,1:T(8,128)(2,1)} %bitcast.7) | data formatting | bytes 4194304 | tf_op jit(solution)/shard_map/transpose | solution.py:248

commit v3 on v2

--- a/solution.py
+++ b/solution.py
@@ -16,11 +16,11 @@
     return lax.dot_general(left, right, (((1,), (0,)), ((), ())), preferred_element_type=jnp.float32)
 
 
-def kernel(n, shards, x, metric, vrow, occ, plan, y, mvm, recv, blocks, own_t, exch, vsum, amp, dens,
-           msem, in_send, in_recv, in_local, g_send, g_recv, f_send, f_recv, out_send, out_recv, out_local):
+def kernel(n, shards, width, raw, metric, vrow, occ, plan, y, held, x, mvm, recv, blocks, own_t, exch, vsum, amp, dens,
+           msem, raw_sem, in_send, in_recv, in_local, g_send, g_recv, f_send, f_recv, out_send, out_recv, out_local):
     grp = lax.axis_index("grp")
     me = lax.axis_index("aux")
-    chunks, rows, width = x.shape[1], x.shape[2], x.shape[3]
+    rows, chunks = raw.shape[0], raw.shape[2] // width
     aux_rows = metric.shape[0]
     nvirt = vrow.shape[1]
     relay = n == 4
@@ -38,6 +38,12 @@
         target = [lax.rem(grp + d, n) for d in range(n)]
         source = [lax.rem(grp + n - d, n) for d in range(n)]
 
+    def raw_copy(k):
+        part = pl.ds(k * width, width)
+        return pltpu.make_async_copy(raw.at[:, :, part], held.at[k], raw_sem.at[k])
+
+    for k in range(chunks):
+        raw_copy(k).start()
     load = pltpu.make_async_copy(metric, mvm, msem)
     load.start()
 
@@ -111,9 +117,11 @@
 
     tile = min(512, aux_rows)
     for k in range(chunks):
+        raw_copy(k).wait()
+        x[:, k] = jnp.swapaxes(held[k].astype(jnp.float32), 0, 1).astype(jnp.bfloat16)
+        if k < WINDOW:
+            send_step(k)
         in_own(k).start()
-    for i in range(WINDOW):
-        send_step(i)
     vsum[...] = vrow[...] + jnp.broadcast_to(vrow[...], (nvirt, nvirt)).T
 
     @pl.when(parity == 1)
@@ -216,18 +224,19 @@
     aux_rows = metric.shape[0]
     width = CHUNK if nvirt % CHUNK == 0 else nvirt
     chunks = nvirt // width
-    x = integrals.reshape(rows, shards, chunks, width).transpose(1, 2, 0, 3)
     any_space = pl.BlockSpec(memory_space=pl.ANY)
     vmem = pl.BlockSpec(memory_space=pltpu.VMEM)
     smem = pl.BlockSpec(memory_space=pltpu.SMEM)
     dma = pltpu.SemaphoreType.DMA
     flops = 2 * aux_rows * nvirt * (aux_rows + 2 * n * nvirt)
     y = pl.pallas_call(
-        functools.partial(kernel, n, shards),
+        functools.partial(kernel, n, shards, width),
         out_shape=jax.ShapeDtypeStruct((shards, rows, nvirt), jnp.bfloat16),
         in_specs=[any_space, any_space, vmem, smem, smem],
         out_specs=any_space,
         scratch_shapes=[
+            pltpu.VMEM((chunks, rows, shards, width), jnp.bfloat16),
+            pltpu.VMEM((shards, chunks, rows, width), jnp.bfloat16),
             pltpu.VMEM((aux_rows, aux_rows), jnp.bfloat16),
             pltpu.VMEM((chunks, shards, rows, width), jnp.bfloat16),
             pltpu.VMEM((n, chunks, aux_rows, width), jnp.bfloat16),
@@ -236,7 +245,7 @@
             pltpu.VMEM((nvirt, nvirt), jnp.float32),
             pltpu.VMEM((n * nvirt, nvirt), jnp.bfloat16),
             pltpu.VMEM((shards, rows, nvirt), jnp.bfloat16),
-            dma, dma((chunks, shards)), dma((chunks, shards)), dma((chunks,)),
+            dma, dma((chunks,)), dma((chunks, shards)), dma((chunks, shards)), dma((chunks,)),
             dma((n, chunks)), dma((n, chunks)), dma((2, chunks)), dma((2, chunks)),
             dma((shards,)), dma((shards,)), dma,
         ],
@@ -244,7 +253,7 @@
             collective_id=0, has_side_effects=True, vmem_limit_bytes=56 * 1024 * 1024),
         cost_estimate=pl.CostEstimate(
             flops=flops, bytes_accessed=2 * aux_rows * aux_rows, transcendentals=0),
-    )(x, metric, virtual_energy.reshape(1, nvirt), occupied_energy, plan)
+    )(integrals, metric, virtual_energy.reshape(1, nvirt), occupied_energy, plan)
     return y.transpose(1, 0, 2)
 
 

time: 128 us -> 125 us (0.977)
  local copies, waits for them, and re-layouts: 7.79 us -> 4.07 us
    reshape x1 -> x0, local copies, waits for them, and re-layouts: 3.72 us -> none  [body(): x = integrals.reshape(rows, shards, chunks, width).transpose(1, 2, 0, 3)]
where the time goes in v3:
time: 125 us
  Pallas kernels  121 us (97%)
  local copies, waits for them, and re-layouts  4.07 us (3%)
    pallas_call x1, Pallas kernels, body(): pl.pallas_call(functools.partial(kernel, n, shards, width), out_shape=jax...  121 us
    transpose x1, local copies, waits for them, and re-layouts, body(): return y.transpose(1, 0, 2)  4.07 us

profile of v3, /device:TPU:0, one launch (start us, length us, event | category | flops | bytes accessed | tf_op | source)
XLA Modules:
  0.0 124.7 jit_solution(16337257130513759156)
XLA Ops:
  0.0 120.6 %shard_map.55 = bf16[8,256,512]{2,1,0:T(8,128)(2,1)} custom-call(bf16[256,8,512]{2,1,0:T(8,128)(2,1)} %raw.1, bf16[2048,2048]{1,0:T(8,128)(2,1)} %metric.1, f32[1,512]{1,0:T(1,128)} %bitcast.3, f32[32]{0:T(128)} %occ.1, s32[4,8]{1,0:T(4,128)} %plan.1), custom_call_target="tpu_custom_call" | custom-call | flops 12884901888 | bytes 8388608 | tf_op jit(solution)/shard_map/pallas_call | solution.py:232
  120.6 4.1 %copy.6 = bf16[256,8,512]{2,1,0:T(8,128)(2,1)} copy(bf16[256,8,512]{2,0,1:T(8,128)(2,1)} %bitcast.2) | data formatting | bytes 4194304 | tf_op jit(solution)/shard_map/transpose | solution.py:257

commit v4 on v3

--- a/solution.py
+++ b/solution.py
@@ -151,9 +151,11 @@
             forward(k - 1)
         own_t[k * width:(k + 1) * width, :] = blocks[0, k].T
 
-    def pair(d):
+    def pair(d, ready=lambda k: None):
         per = max(1, min(256 // width, chunks))
         for k in range(0, chunks, per):
+            for m in range(per):
+                ready(k + m)
             right = jnp.concatenate([blocks[d, k + m] for m in range(per)], axis=1)
             exch[:, k * width:(k + per) * width] = dot(own_t[...], right)
         weight = jnp.float32(0.0)
@@ -170,10 +172,12 @@
         forward(chunks - 1)
         pair(1)
         pair(2)
-        for k in range(chunks):
+
+        def ready(k):
             for way in (0, 1):
                 f_copy(k, way).wait_recv()
-        pair(3)
+
+        pair(3, ready)
     else:
         for d in direct:
             for k in range(chunks):

time: 125 us -> 125 us (level)
  no operation moved by 1% of the time
where the time goes in v4:
time: 125 us; the launch traced here: 124 us
  Pallas kernels  120 us (96%)
  local copies, waits for them, and re-layouts  4.07 us (3%)
    pallas_call x1, Pallas kernels, body(): pl.pallas_call(functools.partial(kernel, n, shards, width), out_shape=jax...  120 us
    transpose x1, local copies, waits for them, and re-layouts, body(): return y.transpose(1, 0, 2)  4.07 us

profile of v4, /device:TPU:0, one launch (start us, length us, event | category | flops | bytes accessed | tf_op | source)
XLA Modules:
  0.0 124.5 jit_solution(12426999538018845350)
XLA Ops:
  0.0 120.4 %shard_map.55 = bf16[8,256,512]{2,1,0:T(8,128)(2,1)} custom-call(bf16[256,8,512]{2,1,0:T(8,128)(2,1)} %raw.1, bf16[2048,2048]{1,0:T(8,128)(2,1)} %metric.1, f32[1,512]{1,0:T(1,128)} %bitcast.3, f32[32]{0:T(128)} %occ.1, s32[4,8]{1,0:T(4,128)} %plan.1), custom_call_target="tpu_custom_call" | custom-call | flops 12884901888 | bytes 8388608 | tf_op jit(solution)/shard_map/pallas_call | solution.py:236
  120.4 4.1 %copy.6 = bf16[256,8,512]{2,1,0:T(8,128)(2,1)} copy(bf16[256,8,512]{2,0,1:T(8,128)(2,1)} %bitcast.2) | data formatting | bytes 4194304 | tf_op jit(solution)/shard_map/transpose | solution.py:261

commit v5 on v4

--- a/solution.py
+++ b/solution.py
@@ -9,7 +9,7 @@
 
 MESH = pl.DeviceIdType.MESH
 CHUNK = 128
-WINDOW = 3
+WINDOW = 4
 
 
 def dot(left, right):

time: 125 us -> 125 us (level)
  no operation moved by 1% of the time
where the time goes in v5:
time: 125 us
  Pallas kernels  120 us (96%)
  local copies, waits for them, and re-layouts  4.07 us (3%)
    pallas_call x1, Pallas kernels, body(): pl.pallas_call(functools.partial(kernel, n, shards, width), out_shape=jax...  120 us
    transpose x1, local copies, waits for them, and re-layouts, body(): return y.transpose(1, 0, 2)  4.07 us

profile of v5, /device:TPU:0, one launch (start us, length us, event | category | flops | bytes accessed | tf_op | source)
XLA Modules:
  0.0 124.5 jit_solution(15698260212828243070)
XLA Ops:
  0.0 120.5 %shard_map.55 = bf16[8,256,512]{2,1,0:T(8,128)(2,1)} custom-call(bf16[256,8,512]{2,1,0:T(8,128)(2,1)} %raw.1, bf16[2048,2048]{1,0:T(8,128)(2,1)} %metric.1, f32[1,512]{1,0:T(1,128)} %bitcast.3, f32[32]{0:T(128)} %occ.1, s32[4,8]{1,0:T(4,128)} %plan.1), custom_call_target="tpu_custom_call" | custom-call | flops 12884901888 | bytes 8388608 | tf_op jit(solution)/shard_map/pallas_call | solution.py:236
  120.5 4.1 %copy.6 = bf16[256,8,512]{2,1,0:T(8,128)(2,1)} copy(bf16[256,8,512]{2,0,1:T(8,128)(2,1)} %bitcast.2) | data formatting | bytes 4194304 | tf_op jit(solution)/shard_map/transpose | solution.py:261
